TPU v7x, 32 devices: a whole 2x2x4 slice. The times are simulated.
32 devices in a mesh: dp: 4 (over x, core), space: 8 (over z, y).
Axes of the slice: x: 2, y: 2, z: 4, core: 2. Of those that a mesh axis runs over, the one named last changes fastest.
Arguments:
- features: bfloat16 [4, 32, 256, 512], P('dp', None, 'space'), may hold values from -6 to 6
- cotangent: bfloat16 [4, 32, 256, 512], P('dp', None, 'space'), may hold values from -6 to 6
- conv_kernel: float32 [7, 7, 512], replicated, may hold values from -0.875 to 0.875
- conv_bias: float32 [512], replicated, may hold values from -3 to 3
- norm_gain: float32 [512], replicated, may hold values from 0.5 to 1.5
- norm_bias: float32 [512], replicated, may hold values from -3 to 3
- weight_in: bfloat16 [512, 2048], P(('dp', 'space')), may hold values from -0.25 to 0.25
- bias_in: float32 [2048], replicated, may hold values from -3 to 3
- weight_out: bfloat16 [2048, 512], P(('dp', 'space')), may hold values from -0.125 to 0.125
- bias_out: float32 [512], replicated, may hold values from -3 to 3
- layer_scale: float32 [512], replicated, may hold values from 0.3 to 1.5
Outputs:
- block_out: bfloat16 [4, 32, 256, 512], P('dp', None, 'space')
- grad_features: bfloat16 [4, 32, 256, 512], P('dp', None, 'space')
- grad_kernel: float32 [7, 7, 512], replicated
- grad_convbias: float32 [512], replicated
- grad_gain: float32 [512], replicated
- grad_normbias: float32 [512], replicated
- grad_inproj: float32 [512, 2048], P(('dp', 'space'))
- grad_inbias: float32 [2048], replicated
- grad_outproj: float32 [2048, 512], P(('dp', 'space'))
- grad_outbias: float32 [512], replicated
- grad_scale: float32 [512], replicated
All inputs are finite; a program needn't handle non-finite values.
Results may differ from a plain program's by a relative error of at most 0.009.
Values may be sent and summed in bfloat16 or wider, within the bound.
A program may use at most 576 MiB of HBM per device.

v0:
```python
import jax
import jax.numpy as jnp
from jax import lax
from jax.sharding import PartitionSpec as P

KS = 7
NORM_EPS = 1e-06


def padded_2(x, sides, width):
    for axis, dim in sides:
        peers, length = (lax.axis_size(axis), x.shape[dim])
        up = [(i, (i + 1) % peers) for i in range(peers - 1)]
        down = [(j, i) for i, j in up]
        last = lax.slice_in_dim(x, length - width, length, axis=dim)
        initial = lax.slice_in_dim(x, 0, width, axis=dim)
        before = lax.ppermute(last, axis, up)
        after = lax.ppermute(initial, axis, down)
        x = jnp.concatenate([before, x, after], axis=dim)
    return x


def gelu_exact(inputs):
    return jax.nn.gelu(inputs, approximate=False)


def conv_forward(padded, kernel, offset, row_count, col_count):
    summed = jnp.zeros((row_count, col_count, padded.shape[2]), jnp.float32)
    for tap_row in range(KS):
        for tap_col in range(KS):
            window = padded[tap_row : tap_row + row_count, tap_col : tap_col + col_count].astype(
                jnp.float32
            )
            summed = summed + kernel[tap_row, tap_col] * window
    return (summed + offset).astype(jnp.bfloat16)


def conv_backward(grad_padded, kernel, row_count, col_count):
    summed = jnp.zeros((row_count, col_count, grad_padded.shape[2]), jnp.float32)
    for tap_row in range(KS):
        for tap_col in range(KS):
            row_start = KS - 1 - tap_row
            col_start = KS - 1 - tap_col
            window = grad_padded[
                row_start : row_start + row_count, col_start : col_start + col_count
            ].astype(jnp.float32)
            summed = summed + kernel[tap_row, tap_col] * window
    return summed


def kernel_gradient(grad_conv, padded, row_count, col_count):
    grad_wide = grad_conv.astype(jnp.float32)
    taps = []
    for tap_row in range(KS):
        tap_line = []
        for tap_col in range(KS):
            window = padded[tap_row : tap_row + row_count, tap_col : tap_col + col_count].astype(
                jnp.float32
            )
            tap_line.append(jnp.sum(grad_wide * window, axis=(0, 1)))
        taps.append(jnp.stack(tap_line))
    return jnp.stack(taps)


def norm_mlp(
    conv_out,
    source,
    upstream,
    norm_gain,
    norm_bias,
    weight_in,
    bias_in,
    weight_out,
    bias_out,
    layer_scale,
):
    widened = conv_out.astype(jnp.float32)
    center = jnp.mean(widened, axis=-1, keepdims=True)
    shifted = widened - center
    inv_std = lax.rsqrt(jnp.mean(shifted * shifted, axis=-1, keepdims=True) + NORM_EPS)
    normed = shifted * inv_std
    activated = (normed * norm_gain + norm_bias).astype(jnp.bfloat16)
    pre_act = jnp.dot(activated, weight_in, preferred_element_type=jnp.float32) + bias_in
    hidden_wide, gelu_back = jax.vjp(gelu_exact, pre_act)
    hidden = hidden_wide.astype(jnp.bfloat16)
    branch = jnp.dot(hidden, weight_out, preferred_element_type=jnp.float32) + bias_out
    block_out = (source.astype(jnp.float32) + layer_scale * branch).astype(jnp.bfloat16)
    upstream_wide = upstream.astype(jnp.float32)
    d_branch = layer_scale * upstream_wide
    d_branch_b = d_branch.astype(jnp.bfloat16)
    grad_scale = jnp.sum(upstream_wide * branch, axis=0)
    grad_outbias = jnp.sum(d_branch, axis=0)
    grad_outproj = lax.dot_general(
        hidden, d_branch_b, (((0,), (0,)), ((), ())), preferred_element_type=jnp.float32
    )
    d_hidden = lax.dot_general(
        d_branch_b, weight_out, (((1,), (1,)), ((), ())), preferred_element_type=jnp.float32
    )
    d_pre = gelu_back(d_hidden)[0]
    d_pre_b = d_pre.astype(jnp.bfloat16)
    grad_inbias = jnp.sum(d_pre, axis=0)
    grad_inproj = lax.dot_general(
        activated, d_pre_b, (((0,), (0,)), ((), ())), preferred_element_type=jnp.float32
    )
    d_act = lax.dot_general(
        d_pre_b, weight_in, (((1,), (1,)), ((), ())), preferred_element_type=jnp.float32
    )
    grad_gain = jnp.sum(d_act * normed, axis=0)
    grad_normbias = jnp.sum(d_act, axis=0)
    scaled = d_act * norm_gain
    grad_conv = inv_std * (
        scaled
        - jnp.mean(scaled, axis=-1, keepdims=True)
        - normed * jnp.mean(scaled * normed, axis=-1, keepdims=True)
    )
    return (
        block_out,
        grad_conv.astype(jnp.bfloat16),
        (
            grad_gain,
            grad_normbias,
            grad_inproj,
            grad_inbias,
            grad_outproj,
            grad_outbias,
            grad_scale,
        ),
    )


def local(
    features,
    cotangent,
    conv_kernel,
    conv_bias,
    norm_gain,
    norm_bias,
    weight_in,
    bias_in,
    weight_out,
    bias_out,
    layer_scale,
):
    reach = KS // 2
    source = features[0]
    upstream = cotangent[0]
    row_count, col_count, channels = source.shape
    full_in, full_out = (
        lax.all_gather(weight_in, ("dp", "space"), axis=0, tiled=True),
        lax.all_gather(weight_out, ("dp", "space"), axis=0, tiled=True),
    )
    rimmed = padded_2(source, (("space", 1),), reach)
    padded = jnp.pad(rimmed, ((reach, reach), (0, 0), (0, 0)))
    conv_out = conv_forward(padded, conv_kernel, conv_bias, row_count, col_count)
    block_out, grad_conv, partials = norm_mlp(
        conv_out.reshape(-1, channels),
        source.reshape(-1, channels),
        upstream.reshape(-1, channels),
        norm_gain,
        norm_bias,
        full_in,
        bias_in,
        full_out,
        bias_out,
        layer_scale,
    )
    grad_conv = grad_conv.reshape(row_count, col_count, channels)
    grad_rimmed = padded_2(grad_conv, (("space", 1),), reach)
    grad_padded = jnp.pad(grad_rimmed, ((reach, reach), (0, 0), (0, 0)))
    conv_back = conv_backward(grad_padded, conv_kernel, row_count, col_count)
    grad_kern = kernel_gradient(grad_conv, padded, row_count, col_count)
    grad_cbias = jnp.sum(grad_conv.astype(jnp.float32), axis=(0, 1))
    grad_feat = (upstream.astype(jnp.float32) + conv_back).astype(jnp.bfloat16)
    grad_gain, grad_normbias, grad_inproj, grad_inbias, grad_outproj, grad_outbias, grad_scale = (
        partials
    )
    reduced = lax.psum(
        (grad_kern, grad_cbias, grad_gain, grad_normbias, grad_inbias, grad_outbias, grad_scale),
        ("dp", "space"),
    )
    owned_in, owned_out = (
        lax.psum_scatter(grad_inproj, ("dp", "space"), scatter_dimension=0, tiled=True),
        lax.psum_scatter(grad_outproj, ("dp", "space"), scatter_dimension=0, tiled=True),
    )
    return (
        block_out.reshape(1, row_count, col_count, channels),
        grad_feat[None],
        reduced[0],
        reduced[1],
        reduced[2],
        reduced[3],
        owned_in,
        reduced[4],
        owned_out,
        reduced[5],
        reduced[6],
    )


def solution(mesh):
    return jax.shard_map(
        local,
        mesh=mesh,
        in_specs=(
            P("dp", None, "space", None),
            P("dp", None, "space", None),
            P(),
            P(),
            P(),
            P(),
            P(("dp", "space"), None),
            P(),
            P(("dp", "space"), None),
            P(),
            P(),
        ),
        out_specs=(
            P("dp", None, "space", None),
            P("dp", None, "space", None),
            P(),
            P(),
            P(),
            P(),
            P(("dp", "space"), None),
            P(),
            P(("dp", "space"), None),
            P(),
            P(),
        ),
        check_vma=False,
    )
```

profile of v0, /device:TPU:0, one launch (start us, length us, event | category | flops | bytes accessed | tf_op | source)
XLA Modules:
  0.0 583.8 jit_solution(10404483312146317047)
XLA Ops:
  8.0 1.1 fusion.152
  9.1 4.9 collective-permute-start
  14.0 1.3 collective-permute-start.1
  15.4 1.2 fusion.153
  16.5 1.1 fusion.154
  17.6 1.0 fusion.155
  18.6 2.3 collective-permute-done.1
  20.9 2.0 select_maximum_fusion.2
  22.9 16.5 %convert_reduce_fusion.1 = (f32[32,32]{1,0:T(8,128)S(1)}, bf16[32,32,512]{2,1,0:T(8,128)(2,1)}) fusion(f32[512]{0:T(512)S(1)} %copy-done.8, bf16[38,38,512]{2,1,0:T(8,128)(2,1)S(1)} %select_maximum_fusion.2, f32[512]{0:T(512)S(1)} %bitcast.310, f32[512]{0:T(512)S(1)} %bitcast.312, f32[512]{0:T(512)S(1)} %bitcast.218, f32[512]{0:T(512)S(1)} %bitcast.220, ...), kind=kLoop, calls=%fused_computation.278 | loop fusion | flops 88079360 | bytes 46440448 | tf_op jit(solution)/shard_map/reduce_sum | solution.py:78
  39.5 1.7 multiply_reduce_fusion.2
  41.3 2.7 add_convert_fusion
  44.1 26.3 %all-gather.3.cloned.1.call-done = bf16[512,2048]{1,0:T(8,128)(2,1)} async-done(((bf16[16,2048]{1,0:T(8,128)(2,1)}), bf16[512,2048]{1,0:T(8,128)(2,1)}) %all-gather.3.cloned.1.call-update) | async-done | bytes 2097168 | tf_op jit(solution)/shard_map/all_gather | solution.py:149
  70.3 23.4 %multiply_convert_fusion = (bf16[1024,2048]{1,0:T(8,128)(2,1)}, f32[1024,2048]{1,0:T(8,128)}, f32[1024,2048]{1,0:T(8,128)}) fusion(f32[2048]{0:T(1024)S(1)} %copy-done.13, bf16[1024,512]{1,0:T(8,128)(2,1)} %add_convert_fusion, bf16[512,2048]{1,0:T(8,128)(2,1)} %all-gather.3.cloned.1.call-done), kind=kOutput, calls=%fused_computation.52 | convolution fusion | flops 2285895680 | bytes 24125440 | tf_op jit(solution)/shard_map/dot_general | solution.py:83
  93.7 35.0 %all-gather.5.cloned.1.call-done = bf16[2048,512]{1,0:T(8,128)(2,1)} async-done(((bf16[64,512]{1,0:T(8,128)(2,1)}), bf16[2048,512]{1,0:T(8,128)(2,1)}) %all-gather.5.cloned.1.call-update) | async-done | bytes 2097168 | tf_op jit(solution)/shard_map/all_gather | solution.py:150
  128.7 6.9 %fusion.134 = (f32[512]{0:T(512)S(1)}, bf16[1024,512]{1,0:T(8,128)(2,1)}, bf16[1024,512]{1,0:T(8,128)(2,1)S(1)}) fusion(bf16[1,32,32,512]{3,2,1,0:T(8,128)(2,1)} %param.12, f32[512]{0:T(512)S(1)} %copy-done.14, f32[512]{0:T(512)S(1)} %copy-done.9, bf16[1,32,32,512]{3,2,1,0:T(8,128)(2,1)S(1)} %copy-done, bf16[1024,2048]{1,0:T(8,128)(2,1)} %get-tuple-element.81, ...), kind=kOutput, calls=%fused_computation.251 | convolution fusion | flops 2152726016 | bytes 10491904 | tf_op jit(solution)/shard_map/dot_general | solution.py:86
  135.6 8.0 %fusion.156 = (f32[2048]{0:T(1024)S(1)}, bf16[1024,2048]{1,0:T(8,128)(2,1)S(1)}) fusion(f32[1024,2048]{1,0:T(8,128)S(1)} %copy-done.16, bf16[1024,512]{1,0:T(8,128)(2,1)S(1)} %get-tuple-element.87, bf16[2048,512]{1,0:T(8,128)(2,1)S(1)} %copy-done.12, f32[1024,2048]{1,0:T(8,128)} %get-tuple-element.141, f32[2048]{0:T(1024)S(1)} %copy-done.13), kind=kOutput, calls=%fused_computation.316 | convolution fusion | flops 2181036032 | bytes 24133632 | tf_op jit(solution)/shard_map/dot_general | solution.py:96
  143.7 2.9 multiply_reduce_fusion
  146.6 6.6 %fusion.129 = (f32[512]{0:T(512)S(1)}, f32[512]{0:T(512)S(1)}, f32[512]{0:T(512)S(1)}, f32[512]{0:T(512)S(1)}, f32[512]{0:T(512)S(1)}, /*index=5*/f32[512]{0:T(5...) fusion(bf16[38,38,512]{2,1,0:T(8,128)(2,1)S(1)} %select_maximum, ...), kind=kLoop, calls=%fused_computation.242 | loop fusion | flops 33545216 | bytes 23123968 | tf_op jit(solution)/shard_map/reduce_sum | solution.py:60
  153.6 5.2 fusion.111
  158.8 4.2 fusion.108
  164.3 6.8 %fusion.157 = f32[2048,512]{1,0:T(8,128)} fusion(bf16[1024,2048]{1,0:T(8,128)(2,1)} %get-tuple-element.81, bf16[1024,512]{1,0:T(8,128)(2,1)} %copy-done.15), kind=kOutput, calls=%fused_computation.317 | convolution fusion | flops 2147483648 | bytes 9437184 | tf_op jit(solution)/shard_map/dot_general | solution.py:93
  171.2 1.2 copy-done.4
  172.4 6.6 %fusion.136 = f32[512,2048]{1,0:T(8,128)} fusion(bf16[1024,512]{1,0:T(8,128)(2,1)S(1)} %copy-done.4, bf16[1024,2048]{1,0:T(8,128)(2,1)} %copy-done.3), kind=kOutput, calls=%fused_computation.257 | convolution fusion | flops 2147483648 | bytes 9437184 | tf_op jit(solution)/shard_map/dot_general | solution.py:102
  179.1 3.5 collective-permute-start.2
  182.6 1.3 collective-permute-start.3
  184.2 41.0 %all-reduce.2 = (f32[512]{0:T(512)}, f32[512]{0:T(512)}, f32[512]{0:T(512)}, f32[2048]{0:T(1024)}, f32[512]{0:T(512)}, /*index=5*/f32[512]{0:T(512)}) all-reduce(f32[512]{0:T(512)S(1)} %get-tuple-element.66, f32[512]{0:T(512)S(1)} %get-tuple-element.11, ...), channel_id=1, replica_groups=mesh['dp'=4,'space'=8] {'dp','space'}, use_global_device_ids=true, to_apply=%region_55.56 | all-reduce | flops 4608 | bytes 36864 | tf_op jit(solution)/shard_map/psum | solution.py:177
  225.2 0.8 select_maximum_fusion
  226.0 16.7 %fusion.149 = bf16[1,32,32,512]{3,2,1,0:T(8,128)(2,1)} fusion(bf16[38,38,512]{2,1,0:T(8,128)(2,1)S(1)} %select_maximum_fusion, f32[512]{0:T(512)S(1)} %bitcast.311, f32[512]{0:T(512)S(1)} %bitcast.313, f32[512]{0:T(512)S(1)} %bitcast.219, f32[512]{0:T(512)S(1)} %bitcast.221, f32[512]{0:T(512)S(1)} %bitcast.223, f32[512]{0:T(512)S(1)} %bitcast.225, ...), kind=kLoop, calls=%fused_computation.299 | loop fusion | flops 87556096 | bytes 47482880 | tf_op jit(solution)/shard_map/broadcast_in_dim | solution.py:187
  242.7 41.1 %all-reduce.5.cloned.1.call-done = f32[7,7,512]{2,1,0:T(8,128)} async-done(((f32[7,7,512]{2,1,0:T(8,128)}), f32[7,7,512]{2,1,0:T(8,128)}) %all-reduce.5.cloned.1.call-update) | async-done | bytes 100368 | tf_op jit(solution)/shard_map/psum | solution.py:177
  283.8 147.9 %reduce-scatter.5.cloned.1.call-done = f32[64,512]{1,0:T(8,128)} async-done(((f32[2048,512]{1,0:T(8,128)}), f32[64,512]{1,0:T(8,128)}) %reduce-scatter.5.cloned.1.call-update) | async-done | bytes 131088 | tf_op jit(solution)/shard_map/reduce_scatter | solution.py:183
  431.7 144.1 %reduce-scatter.3.cloned.1.call-done = f32[16,2048]{1,0:T(8,128)} async-done(((f32[512,2048]{1,0:T(8,128)}), f32[16,2048]{1,0:T(8,128)}) %reduce-scatter.3.cloned.1.call-update) | async-done | bytes 131088 | tf_op jit(solution)/shard_map/reduce_scatter | solution.py:182
  575.8 1.6 copy.29
  (68 shorter events, 3.2 us)
Async XLA Ops:
  7.2 15.7 %copy-start = (bf16[1,32,32,512]{3,2,1,0:T(8,128)(2,1)S(1)}, bf16[1,32,32,512]{3,2,1,0:T(8,128)(2,1)}, u32[]{:S(2)}) copy-start(bf16[1,32,32,512]{3,2,1,0:T(8,128)(2,1)} %param.11) | copy-start | bytes 3145732
  7.2 15.7 %copy-start.8 = (f32[512]{0:T(512)S(1)}, f32[512]{0:T(512)}, u32[]{:S(2)}) copy-start(f32[512]{0:T(512)} %param.14) | copy-start | bytes 6148
  7.2 63.1 %all-gather.3.cloned.1.call-start = ((), (), s32[]{:S(2)}) async-start(), calls=%async_computation.2 | async-start | bytes 2162688 | tf_op jit(solution)/shard_map/all_gather | solution.py:149
  7.9 120.8 %all-gather.5.cloned.1.call-start = ((), (), s32[]{:S(2)}) async-start(), calls=%async_computation.3 | async-start | bytes 2162688 | tf_op jit(solution)/shard_map/all_gather | solution.py:150
  9.1 9.5 %collective-permute-start = (bf16[32,3,512]{2,1,0:T(4,128)(2,1)S(1)}, bf16[32,3,512]{2,1,0:T(4,128)(2,1)S(1)}, u32[]{:S(2)}, u32[]{:S(2)}) collective-permute-start(bf16[32,3,512]{2,1,0:T(4,128)(2,1)S(1)} %get-tuple-element.90), channel_id=1, source_target_pairs={{0,1},{1,2},{2,3},{3,4},{4,5},{5,6},{6,7},{8,9},{9,10},{10,11},{11... | collective-permute-start | bytes 294920 | tf_op jit(solution)/shard_map/ppermute | solution.py:17
  14.0 6.9 %collective-permute-start.1 = (bf16[32,3,512]{2,1,0:T(4,128)(2,1)S(1)}, bf16[32,3,512]{2,1,0:T(4,128)(2,1)S(1)}, u32[]{:S(2)}, u32[]{:S(2)}) collective-permute-start(bf16[32,3,512]{2,1,0:T(4,128)(2,1)S(1)} %get-tuple-element.91), channel_id=1, source_target_pairs={{1,0},{2,1},{3,2},{4,3},{5,4},{6,5},{7,6},{9,8},{10,9},{11,10},{12... | collective-permute-start | bytes 294920 | tf_op jit(solution)/shard_map/ppermute | solution.py:18
  15.3 268.5 %all-reduce.5.cloned.1.call-start = ((), (), s32[]{:S(2)}) async-start(), calls=%async_computation.4 | async-start | bytes 229376 | tf_op jit(solution)/shard_map/psum | solution.py:177
  22.9 18.4 %copy-start.7 = (f32[512]{0:T(512)S(1)}, f32[512]{0:T(512)}, u32[]{:S(2)}) copy-start(f32[512]{0:T(512)} %param.15) | copy-start | bytes 6148
  22.9 18.4 %copy-start.10 = (f32[512]{0:T(512)S(1)}, f32[512]{0:T(512)}, u32[]{:S(2)}) copy-start(f32[512]{0:T(512)} %param.16) | copy-start | bytes 6148
  39.4 30.9 %copy-start.13 = (f32[2048]{0:T(1024)S(1)}, f32[2048]{0:T(1024)}, u32[]{:S(2)}) copy-start(f32[2048]{0:T(1024)} %param.18) | copy-start | bytes 24580
  44.1 84.7 %copy-start.9 = (f32[512]{0:T(512)S(1)}, f32[512]{0:T(512)}, u32[]{:S(2)}) copy-start(f32[512]{0:T(512)} %param.21) | copy-start | bytes 6148
  44.1 84.7 %copy-start.14 = (f32[512]{0:T(512)S(1)}, f32[512]{0:T(512)}, u32[]{:S(2)}) copy-start(f32[512]{0:T(512)} %param.20) | copy-start | bytes 6148
  128.7 6.9 %copy-start.12 = (bf16[2048,512]{1,0:T(8,128)(2,1)S(1)}, bf16[2048,512]{1,0:T(8,128)(2,1)}, u32[]{:S(2)}) copy-start(bf16[2048,512]{1,0:T(8,128)(2,1)} %all-gather.5.cloned.1.call-done) | copy-start | bytes 6291460
  128.7 6.9 %copy-start.16 = (f32[1024,2048]{1,0:T(8,128)S(1)}, f32[1024,2048]{1,0:T(8,128)}, u32[]{:S(2)}) copy-start(f32[1024,2048]{1,0:T(8,128)} %get-tuple-element.82) | copy-start | bytes 25165828
  135.6 8.0 %copy-start.15 = (bf16[1024,512]{1,0:T(8,128)(2,1)}, bf16[1024,512]{1,0:T(8,128)(2,1)S(1)}, u32[]{:S(2)}) copy-start(bf16[1024,512]{1,0:T(8,128)(2,1)S(1)} %get-tuple-element.87) | copy-start | bytes 3145732
  135.6 8.0 %copy-start.2 = (bf16[32,32,512]{2,1,0:T(8,128)(2,1)S(1)}, bf16[32,32,512]{2,1,0:T(8,128)(2,1)}, u32[]{:S(2)}) copy-start(bf16[32,32,512]{2,1,0:T(8,128)(2,1)} %get-tuple-element.84) | copy-start | bytes 3145732
  135.6 8.0 %copy-start.11 = (bf16[512,2048]{1,0:T(8,128)(2,1)S(1)}, bf16[512,2048]{1,0:T(8,128)(2,1)}, u32[]{:S(2)}) copy-start(bf16[512,2048]{1,0:T(8,128)(2,1)} %all-gather.3.cloned.1.call-done) | copy-start | bytes 6291460
  143.6 2.9 copy-start.3
  146.5 6.6 %copy-start.1 = (bf16[1,32,32,512]{3,2,1,0:T(8,128)(2,1)S(1)}, bf16[1,32,32,512]{3,2,1,0:T(8,128)(2,1)}, u32[]{:S(2)}) copy-start(bf16[1,32,32,512]{3,2,1,0:T(8,128)(2,1)} %param.11) | copy-start | bytes 3145732
  163.4 0.6 copy-start.6
  164.0 267.6 %reduce-scatter.5.cloned.1.call-start = ((), (), s32[]{:S(2)}) async-start(), calls=%async_computation.6 | async-start | bytes 4325376 | tf_op jit(solution)/shard_map/reduce_scatter | solution.py:183
  171.1 1.2 copy-start.4
  171.2 404.6 %reduce-scatter.3.cloned.1.call-start = ((), (), s32[]{:S(2)}) async-start(), calls=%async_computation.5 | async-start | bytes 4325376 | tf_op jit(solution)/shard_map/reduce_scatter | solution.py:182
  178.9 4.9 copy-start.5
  179.1 46.1 %collective-permute-start.2 = (bf16[32,3,512]{2,1,0:T(4,128)(2,1)S(1)}, bf16[32,3,512]{2,1,0:T(4,128)(2,1)S(1)}, u32[]{:S(2)}, u32[]{:S(2)}) collective-permute-start(bf16[32,3,512]{2,1,0:T(4,128)(2,1)S(1)} %get-tuple-element.88), channel_id=1, source_target_pairs={{0,1},{1,2},{2,3},{3,4},{4,5},{5,6},{6,7},{8,9},{9,10},{10,11},{11... | collective-permute-start | bytes 294920 | tf_op jit(solution)/shard_map/ppermute | solution.py:17
  182.6 42.6 %collective-permute-start.3 = (bf16[32,3,512]{2,1,0:T(4,128)(2,1)S(1)}, bf16[32,3,512]{2,1,0:T(4,128)(2,1)S(1)}, u32[]{:S(2)}, u32[]{:S(2)}) collective-permute-start(bf16[32,3,512]{2,1,0:T(4,128)(2,1)S(1)} %get-tuple-element.89), channel_id=1, source_target_pairs={{1,0},{2,1},{3,2},{4,3},{5,4},{6,5},{7,6},{9,8},{10,9},{11,10},{12... | collective-permute-start | bytes 294920 | tf_op jit(solution)/shard_map/ppermute | solution.py:18
Sparse Core Ops, SparseCore 0:
  11.0 59.2 all-gather.2
  73.3 55.3 all-gather.4
  164.2 119.5 all-reduce.4
  286.5 145.1 reduce-scatter.4
  434.4 141.3 reduce-scatter.2
where the time goes:
time: 585 us; the launch traced here: 584 us
  waiting for transfers between devices  397 us (68%)
  other arithmetic  57.2 us (10%)
  matrix products  54.5 us (9%)
  blocking collectives  41 us (7%)
  between operations  14.1 us (2%)
  starting transfers between devices  11.4 us (2%)
  local copies, waits for them, and re-layouts  8.29 us (1%)
    reduce_scatter x1, waiting for transfers between devices, local(): lax.psum_scatter(grad_outproj, ('dp', 'space'), scatter_dimension=0, tile...  148 us
    reduce_scatter x1, waiting for transfers between devices, local(): lax.psum_scatter(grad_inproj, ('dp', 'space'), scatter_dimension=0, tiled...  144 us
    psum x1, waiting for transfers between devices, local(): lax.psum((grad_kern, grad_cbias, grad_gain, grad_normbias, grad_inbias, g...  41.1 us
    psum x1, blocking collectives, local(): lax.psum((grad_kern, grad_cbias, grad_gain, grad_normbias, grad_inbias, g...  41 us
    all_gather x1, waiting for transfers between devices, local(): lax.all_gather(weight_out, ('dp', 'space'), axis=0, tiled=True)  35 us
    all_gather x1, waiting for transfers between devices, local(): lax.all_gather(weight_in, ('dp', 'space'), axis=0, tiled=True)  26.3 us
    dot_general x1, matrix products, norm_mlp(): jnp.dot(activated, weight_in, preferred_element_type=jnp.float32) + bias_in  23.4 us
    broadcast_in_dim x1, other arithmetic, local(): grad_feat[None]  16.7 us
  transfers between devices with their start and end apart: 9, of which 6 were waited for; matrix products, arithmetic and copies ran while one was open for 14% of the time, Pallas kernels for 0%

commit v1 on v0

--- a/solution.py
+++ b/solution.py
@@ -174,10 +174,17 @@
     grad_gain, grad_normbias, grad_inproj, grad_inbias, grad_outproj, grad_outbias, grad_scale = (
         partials
     )
-    reduced = lax.psum(
-        (grad_kern, grad_cbias, grad_gain, grad_normbias, grad_inbias, grad_outbias, grad_scale),
-        ("dp", "space"),
-    )
+    reduced = (
+        grad_kern,
+        grad_cbias,
+        grad_gain,
+        grad_normbias,
+        grad_inbias,
+        grad_outbias,
+        grad_scale,
+    )
+    for over in ("space", "dp"):
+        reduced = lax.psum(reduced, over)
     owned_in, owned_out = (
         lax.psum_scatter(grad_inproj, ("dp", "space"), scatter_dimension=0, tiled=True),
         lax.psum_scatter(grad_outproj, ("dp", "space"), scatter_dimension=0, tiled=True),

time: 585 us -> 565 us (0.966)
  waiting for transfers between devices: 397 us -> 369 us
  blocking collectives: 41 us -> 48.8 us
    reduce_scatter x1, waiting for transfers between devices: 148 us -> 93.1 us  [local(): lax.psum_scatter(grad_outproj, ('dp', 'space'), scatter_dimension=0, tile...]
    psum x1 -> x2, waiting for transfers between devices: 41.1 us -> 68 us  [local(): reduced = lax.psum(reduced, over)]
    psum x1 -> x2, blocking collectives: 41 us -> 48.8 us  [local(): reduced = lax.psum(reduced, over)]
  transfers between devices with their start and end apart: 9 -> 10, of which waited for: 6 -> 6; matrix products, arithmetic and copies ran while one was open for 14% -> 15% of each run, Pallas kernels for 0% -> 0%
where the time goes in v1:
time: 565 us
  waiting for transfers between devices  369 us (65%)
  other arithmetic  58.3 us (10%)
  matrix products  54.5 us (10%)
  blocking collectives  48.8 us (9%)
  between operations  14.5 us (3%)
  starting transfers between devices  11.3 us (2%)
  local copies, waits for them, and re-layouts  8.29 us (1%)
    reduce_scatter x1, waiting for transfers between devices, local(): lax.psum_scatter(grad_inproj, ('dp', 'space'), scatter_dimension=0, tiled...  144 us
    reduce_scatter x1, waiting for transfers between devices, local(): lax.psum_scatter(grad_outproj, ('dp', 'space'), scatter_dimension=0, tile...  93.1 us
    psum x2, waiting for transfers between devices, local(): reduced = lax.psum(reduced, over)  68 us
    psum x2, blocking collectives, local(): reduced = lax.psum(reduced, over)  48.8 us
    all_gather x1, waiting for transfers between devices, local(): lax.all_gather(weight_out, ('dp', 'space'), axis=0, tiled=True)  35 us
    all_gather x1, waiting for transfers between devices, local(): lax.all_gather(weight_in, ('dp', 'space'), axis=0, tiled=True)  26.3 us
    dot_general x1, matrix products, norm_mlp(): jnp.dot(activated, weight_in, preferred_element_type=jnp.float32) + bias_in  23.4 us
    broadcast_in_dim x1, other arithmetic, local(): grad_feat[None]  17.8 us
  transfers between devices with their start and end apart: 10, of which 6 were waited for; matrix products, arithmetic and copies ran while one was open for 15% of the time, Pallas kernels for 0%

profile of v1, /device:TPU:0, one launch (start us, length us, event | category | flops | bytes accessed | tf_op | source)
XLA Modules:
  0.0 564.7 jit_solution(11321310373579083791)
XLA Ops:
  8.0 1.1 fusion.152
  9.1 4.9 collective-permute-start
  14.0 1.3 collective-permute-start.1
  15.4 1.2 fusion.153
  16.5 1.1 fusion.154
  17.6 1.0 fusion.155
  18.6 2.3 collective-permute-done.1
  20.9 2.0 select_maximum_fusion.2
  22.9 16.5 %convert_reduce_fusion.1 = (f32[32,32]{1,0:T(8,128)S(1)}, bf16[32,32,512]{2,1,0:T(8,128)(2,1)}) fusion(f32[512]{0:T(512)S(1)} %copy-done.8, bf16[38,38,512]{2,1,0:T(8,128)(2,1)S(1)} %select_maximum_fusion.2, f32[512]{0:T(512)S(1)} %bitcast.310, f32[512]{0:T(512)S(1)} %bitcast.312, f32[512]{0:T(512)S(1)} %bitcast.218, f32[512]{0:T(512)S(1)} %bitcast.220, ...), kind=kLoop, calls=%fused_computation.278 | loop fusion | flops 88079360 | bytes 46440448 | tf_op jit(solution)/shard_map/reduce_sum | solution.py:78
  39.5 1.7 multiply_reduce_fusion.2
  41.3 2.7 add_convert_fusion
  44.1 26.3 %all-gather.3.cloned.1.call-done = bf16[512,2048]{1,0:T(8,128)(2,1)} async-done(((bf16[16,2048]{1,0:T(8,128)(2,1)}), bf16[512,2048]{1,0:T(8,128)(2,1)}) %all-gather.3.cloned.1.call-update) | async-done | bytes 2097168 | tf_op jit(solution)/shard_map/all_gather | solution.py:149
  70.3 23.4 %multiply_convert_fusion = (bf16[1024,2048]{1,0:T(8,128)(2,1)}, f32[1024,2048]{1,0:T(8,128)}, f32[1024,2048]{1,0:T(8,128)}) fusion(f32[2048]{0:T(1024)S(1)} %copy-done.13, bf16[1024,512]{1,0:T(8,128)(2,1)} %add_convert_fusion, bf16[512,2048]{1,0:T(8,128)(2,1)} %all-gather.3.cloned.1.call-done), kind=kOutput, calls=%fused_computation.52 | convolution fusion | flops 2285895680 | bytes 24125440 | tf_op jit(solution)/shard_map/dot_general | solution.py:83
  93.7 35.0 %all-gather.5.cloned.1.call-done = bf16[2048,512]{1,0:T(8,128)(2,1)} async-done(((bf16[64,512]{1,0:T(8,128)(2,1)}), bf16[2048,512]{1,0:T(8,128)(2,1)}) %all-gather.5.cloned.1.call-update) | async-done | bytes 2097168 | tf_op jit(solution)/shard_map/all_gather | solution.py:150
  128.7 6.9 %fusion.134 = (f32[512]{0:T(512)S(1)}, bf16[1024,512]{1,0:T(8,128)(2,1)}, bf16[1024,512]{1,0:T(8,128)(2,1)S(1)}) fusion(bf16[1,32,32,512]{3,2,1,0:T(8,128)(2,1)} %param.12, f32[512]{0:T(512)S(1)} %copy-done.14, f32[512]{0:T(512)S(1)} %copy-done.9, bf16[1,32,32,512]{3,2,1,0:T(8,128)(2,1)S(1)} %copy-done, bf16[1024,2048]{1,0:T(8,128)(2,1)} %get-tuple-element.87, ...), kind=kOutput, calls=%fused_computation.251 | convolution fusion | flops 2152726016 | bytes 10491904 | tf_op jit(solution)/shard_map/dot_general | solution.py:86
  135.6 8.0 %fusion.156 = (f32[2048]{0:T(1024)S(1)}, bf16[1024,2048]{1,0:T(8,128)(2,1)S(1)}) fusion(f32[1024,2048]{1,0:T(8,128)S(1)} %copy-done.16, bf16[1024,512]{1,0:T(8,128)(2,1)S(1)} %get-tuple-element.93, bf16[2048,512]{1,0:T(8,128)(2,1)S(1)} %copy-done.12, f32[1024,2048]{1,0:T(8,128)} %get-tuple-element.147, f32[2048]{0:T(1024)S(1)} %copy-done.13), kind=kOutput, calls=%fused_computation.316 | convolution fusion | flops 2181036032 | bytes 24133632 | tf_op jit(solution)/shard_map/dot_general | solution.py:96
  143.7 2.9 multiply_reduce_fusion
  146.6 6.6 %fusion.129 = (f32[512]{0:T(512)S(1)}, f32[512]{0:T(512)S(1)}, f32[512]{0:T(512)S(1)}, f32[512]{0:T(512)S(1)}, f32[512]{0:T(512)S(1)}, /*index=5*/f32[512]{0:T(5...) fusion(bf16[38,38,512]{2,1,0:T(8,128)(2,1)S(1)} %select_maximum, ...), kind=kLoop, calls=%fused_computation.242 | loop fusion | flops 33545216 | bytes 23123968 | tf_op jit(solution)/shard_map/reduce_sum | solution.py:60
  153.6 5.2 fusion.111
  158.8 4.2 fusion.108
  164.1 68.0 %all-reduce.7.cloned.1.call-done = f32[7,7,512]{2,1,0:T(8,128)} async-done(((f32[7,7,512]{2,1,0:T(8,128)}), f32[7,7,512]{2,1,0:T(8,128)}) %all-reduce.7.cloned.1.call-update) | async-done | bytes 100368 | tf_op jit(solution)/shard_map/psum | solution.py:187
  232.4 6.8 %fusion.157 = f32[2048,512]{1,0:T(8,128)} fusion(bf16[1024,2048]{1,0:T(8,128)(2,1)} %get-tuple-element.87, bf16[1024,512]{1,0:T(8,128)(2,1)} %copy-done.15), kind=kOutput, calls=%fused_computation.317 | convolution fusion | flops 2147483648 | bytes 9437184 | tf_op jit(solution)/shard_map/dot_general | solution.py:93
  239.3 1.2 copy-done.4
  240.4 6.5 %fusion.136 = f32[512,2048]{1,0:T(8,128)} fusion(bf16[1024,512]{1,0:T(8,128)(2,1)S(1)} %copy-done.4, bf16[1024,2048]{1,0:T(8,128)(2,1)} %copy-done.3), kind=kOutput, calls=%fused_computation.257 | convolution fusion | flops 2147483648 | bytes 9437184 | tf_op jit(solution)/shard_map/dot_general | solution.py:102
  247.1 3.4 collective-permute-start.2
  250.5 1.3 collective-permute-start.3
  252.1 37.6 %all-reduce.2 = (f32[512]{0:T(512)S(1)}, f32[512]{0:T(512)S(1)}, f32[512]{0:T(512)S(1)}, f32[2048]{0:T(1024)S(1)}, f32[512]{0:T(512)S(1)}, /*index=5*/f32[512]{0:T(512)S(1)}) all-reduce(f32[512]{0:T(512)S(1)} %get-tuple-element.66, f32[512]{0:T(512)S(1)} %get-tuple-element.11, ...), channel_id=1, replica_groups=mesh['dp'=4,'space'=8] {'space'}, use_global_device_ids=true, to_apply=%region_56.57 | all-reduce | flops 4608 | bytes 36864 | tf_op jit(solution)/shard_map/psum | solution.py:187
  289.7 11.2 %all-reduce.3 = (f32[512]{0:T(512)}, f32[512]{0:T(512)}, f32[512]{0:T(512)}, f32[2048]{0:T(1024)}, f32[512]{0:T(512)}, /*index=5*/f32[512]{0:T(512)}) all-reduce(f32[512]{0:T(512)S(1)} %get-tuple-element.74, f32[512]{0:T(512)S(1)} %get-tuple-element.75, f32[512]{0:T(512)S(1)} %get-tuple-element.76, ...), channel_id=1, replica_groups=mesh['dp'=4,'space'=8] {'dp'}, use_global_device_ids=true, to_apply=%region_57.58 | all-reduce | flops 4608 | bytes 36864 | tf_op jit(solution)/shard_map/psum | solution.py:187
  301.7 17.8 %fusion.149 = bf16[1,32,32,512]{3,2,1,0:T(8,128)(2,1)} fusion(bf16[38,38,512]{2,1,0:T(8,128)(2,1)S(1)} %select_maximum_fusion, f32[512]{0:T(512)S(1)} %bitcast.311, f32[512]{0:T(512)S(1)} %bitcast.313, f32[512]{0:T(512)S(1)} %bitcast.219, f32[512]{0:T(512)S(1)} %bitcast.221, f32[512]{0:T(512)S(1)} %bitcast.223, f32[512]{0:T(512)S(1)} %bitcast.225, ...), kind=kLoop, calls=%fused_computation.299 | loop fusion | flops 87556096 | bytes 47482880 | tf_op jit(solution)/shard_map/broadcast_in_dim | solution.py:194
  319.5 93.1 %reduce-scatter.5.cloned.1.call-done = f32[64,512]{1,0:T(8,128)} async-done(((f32[2048,512]{1,0:T(8,128)}), f32[64,512]{1,0:T(8,128)}) %reduce-scatter.5.cloned.1.call-update) | async-done | bytes 131088 | tf_op jit(solution)/shard_map/reduce_scatter | solution.py:190
  412.5 143.8 %reduce-scatter.3.cloned.1.call-done = f32[16,2048]{1,0:T(8,128)} async-done(((f32[512,2048]{1,0:T(8,128)}), f32[16,2048]{1,0:T(8,128)}) %reduce-scatter.3.cloned.1.call-update) | async-done | bytes 131088 | tf_op jit(solution)/shard_map/reduce_scatter | solution.py:189
  556.3 1.6 copy.30
  (72 shorter events, 4.0 us)
Async XLA Ops:
  7.2 15.7 %copy-start = (bf16[1,32,32,512]{3,2,1,0:T(8,128)(2,1)S(1)}, bf16[1,32,32,512]{3,2,1,0:T(8,128)(2,1)}, u32[]{:S(2)}) copy-start(bf16[1,32,32,512]{3,2,1,0:T(8,128)(2,1)} %param.11) | copy-start | bytes 3145732
  7.2 15.7 %copy-start.8 = (f32[512]{0:T(512)S(1)}, f32[512]{0:T(512)}, u32[]{:S(2)}) copy-start(f32[512]{0:T(512)} %param.14) | copy-start | bytes 6148
  7.2 63.1 %all-gather.3.cloned.1.call-start = ((), (), s32[]{:S(2)}) async-start(), calls=%async_computation.2 | async-start | bytes 2162688 | tf_op jit(solution)/shard_map/all_gather | solution.py:149
  7.9 120.8 %all-gather.5.cloned.1.call-start = ((), (), s32[]{:S(2)}) async-start(), calls=%async_computation.3 | async-start | bytes 2162688 | tf_op jit(solution)/shard_map/all_gather | solution.py:150
  9.1 9.5 %collective-permute-start = (bf16[32,3,512]{2,1,0:T(4,128)(2,1)S(1)}, bf16[32,3,512]{2,1,0:T(4,128)(2,1)S(1)}, u32[]{:S(2)}, u32[]{:S(2)}) collective-permute-start(bf16[32,3,512]{2,1,0:T(4,128)(2,1)S(1)} %get-tuple-element.96), channel_id=1, source_target_pairs={{0,1},{1,2},{2,3},{3,4},{4,5},{5,6},{6,7},{8,9},{9,10},{10,11},{11... | collective-permute-start | bytes 294920 | tf_op jit(solution)/shard_map/ppermute | solution.py:17
  14.0 6.9 %collective-permute-start.1 = (bf16[32,3,512]{2,1,0:T(4,128)(2,1)S(1)}, bf16[32,3,512]{2,1,0:T(4,128)(2,1)S(1)}, u32[]{:S(2)}, u32[]{:S(2)}) collective-permute-start(bf16[32,3,512]{2,1,0:T(4,128)(2,1)S(1)} %get-tuple-element.97), channel_id=1, source_target_pairs={{1,0},{2,1},{3,2},{4,3},{5,4},{6,5},{7,6},{9,8},{10,9},{11,10},{12... | collective-permute-start | bytes 294920 | tf_op jit(solution)/shard_map/ppermute | solution.py:18
  15.3 216.7 %all-reduce.7.cloned.1.call-start = ((), (), s32[]{:S(2)}) async-start(), calls=%async_computation.4 | async-start | bytes 229376 | tf_op jit(solution)/shard_map/psum | solution.py:187
  22.9 18.4 %copy-start.7 = (f32[512]{0:T(512)S(1)}, f32[512]{0:T(512)}, u32[]{:S(2)}) copy-start(f32[512]{0:T(512)} %param.15) | copy-start | bytes 6148
  22.9 18.4 %copy-start.10 = (f32[512]{0:T(512)S(1)}, f32[512]{0:T(512)}, u32[]{:S(2)}) copy-start(f32[512]{0:T(512)} %param.16) | copy-start | bytes 6148
  39.4 30.9 %copy-start.13 = (f32[2048]{0:T(1024)S(1)}, f32[2048]{0:T(1024)}, u32[]{:S(2)}) copy-start(f32[2048]{0:T(1024)} %param.18) | copy-start | bytes 24580
  44.1 84.7 %copy-start.9 = (f32[512]{0:T(512)S(1)}, f32[512]{0:T(512)}, u32[]{:S(2)}) copy-start(f32[512]{0:T(512)} %param.21) | copy-start | bytes 6148
  44.1 84.7 %copy-start.14 = (f32[512]{0:T(512)S(1)}, f32[512]{0:T(512)}, u32[]{:S(2)}) copy-start(f32[512]{0:T(512)} %param.20) | copy-start | bytes 6148
  128.7 6.9 %copy-start.12 = (bf16[2048,512]{1,0:T(8,128)(2,1)S(1)}, bf16[2048,512]{1,0:T(8,128)(2,1)}, u32[]{:S(2)}) copy-start(bf16[2048,512]{1,0:T(8,128)(2,1)} %all-gather.5.cloned.1.call-done) | copy-start | bytes 6291460
  128.7 6.9 %copy-start.16 = (f32[1024,2048]{1,0:T(8,128)S(1)}, f32[1024,2048]{1,0:T(8,128)}, u32[]{:S(2)}) copy-start(f32[1024,2048]{1,0:T(8,128)} %get-tuple-element.88) | copy-start | bytes 25165828
  135.6 8.0 %copy-start.15 = (bf16[1024,512]{1,0:T(8,128)(2,1)}, bf16[1024,512]{1,0:T(8,128)(2,1)S(1)}, u32[]{:S(2)}) copy-start(bf16[1024,512]{1,0:T(8,128)(2,1)S(1)} %get-tuple-element.93) | copy-start | bytes 3145732
  135.6 8.0 %copy-start.2 = (bf16[32,32,512]{2,1,0:T(8,128)(2,1)S(1)}, bf16[32,32,512]{2,1,0:T(8,128)(2,1)}, u32[]{:S(2)}) copy-start(bf16[32,32,512]{2,1,0:T(8,128)(2,1)} %get-tuple-element.90) | copy-start | bytes 3145732
  135.6 8.0 %copy-start.11 = (bf16[512,2048]{1,0:T(8,128)(2,1)S(1)}, bf16[512,2048]{1,0:T(8,128)(2,1)}, u32[]{:S(2)}) copy-start(bf16[512,2048]{1,0:T(8,128)(2,1)} %all-gather.3.cloned.1.call-done) | copy-start | bytes 6291460
  143.6 2.9 copy-start.3
  146.5 6.6 %copy-start.1 = (bf16[1,32,32,512]{3,2,1,0:T(8,128)(2,1)S(1)}, bf16[1,32,32,512]{3,2,1,0:T(8,128)(2,1)}, u32[]{:S(2)}) copy-start(bf16[1,32,32,512]{3,2,1,0:T(8,128)(2,1)} %param.11) | copy-start | bytes 3145732
  163.4 0.6 copy-start.6
  164.0 155.4 %all-reduce.9.cloned.1.call-start = ((), (), s32[]{:S(2)}) async-start(), calls=%async_computation.5 | async-start | bytes 229376 | tf_op jit(solution)/shard_map/psum | solution.py:187
  232.1 180.4 %reduce-scatter.5.cloned.1.call-start = ((), (), s32[]{:S(2)}) async-start(), calls=%async_computation.7 | async-start | bytes 4325376 | tf_op jit(solution)/shard_map/reduce_scatter | solution.py:190
  239.2 1.2 copy-start.4
  239.2 317.1 %reduce-scatter.3.cloned.1.call-start = ((), (), s32[]{:S(2)}) async-start(), calls=%async_computation.6 | async-start | bytes 4325376 | tf_op jit(solution)/shard_map/reduce_scatter | solution.py:189
  247.0 4.8 copy-start.5
  247.1 53.8 %collective-permute-start.2 = (bf16[32,3,512]{2,1,0:T(4,128)(2,1)S(1)}, bf16[32,3,512]{2,1,0:T(4,128)(2,1)S(1)}, u32[]{:S(2)}, u32[]{:S(2)}) collective-permute-start(bf16[32,3,512]{2,1,0:T(4,128)(2,1)S(1)} %get-tuple-element.94), channel_id=1, source_target_pairs={{0,1},{1,2},{2,3},{3,4},{4,5},{5,6},{6,7},{8,9},{9,10},{10,11},{11... | collective-permute-start | bytes 294920 | tf_op jit(solution)/shard_map/ppermute | solution.py:17
  250.5 50.4 %collective-permute-start.3 = (bf16[32,3,512]{2,1,0:T(4,128)(2,1)S(1)}, bf16[32,3,512]{2,1,0:T(4,128)(2,1)S(1)}, u32[]{:S(2)}, u32[]{:S(2)}) collective-permute-start(bf16[32,3,512]{2,1,0:T(4,128)(2,1)S(1)} %get-tuple-element.95), channel_id=1, source_target_pairs={{1,0},{2,1},{3,2},{4,3},{5,4},{6,5},{7,6},{9,8},{10,9},{11,10},{12... | collective-permute-start | bytes 294920 | tf_op jit(solution)/shard_map/ppermute | solution.py:18
Sparse Core Ops, SparseCore 0:
  11.0 59.2 all-gather.2
  73.3 55.3 all-gather.4
  164.2 67.8 all-reduce.6
  234.4 29.7 all-reduce.8
  266.9 145.5 reduce-scatter.4
  415.2 141.0 reduce-scatter.2
